TPU v7x, 128 devices: a whole 4x4x4 slice. The times are simulated.
128 devices in a mesh: blk: 16 (over z, x_hi, core), group: 8 (over y, x_lo).
Axes of the slice: x: 4 (x_hi: 2, x_lo: 2; x = x_hi * 2 + x_lo), y: 4, z: 4, core: 2. Of those that a mesh axis runs over, the one named last changes fastest.
Arguments:
- images: bfloat16 [22528, 1152], P(('blk', 'group')), may hold values from -0.1796875 to 0.1796875
- texts: bfloat16 [22528, 1152], P(('blk', 'group')), may hold values from -0.1796875 to 0.1796875
- match: int32 [22528], P(('blk', 'group')), may hold values from 0 to 22527, each once
- logit_scale: float32 [1], replicated, may hold values from 20 to 40
- logit_bias: float32 [1], replicated, may hold values from -7 to -4
Outputs:
- image_grad: float32 [22528, 1152], P(('blk', 'group'))
- text_grad: float32 [22528, 1152], P(('blk', 'group'))
Inputs may be any that keep to these rules, and one draw needn't show every extreme that they name: match holds each text index exactly once.
All inputs are finite; a program needn't handle non-finite values.
Results may differ from a plain program's by a relative error of at most 0.008.
Values may be sent and summed in bfloat16 or wider, within the bound.
A program may use at most 128 MiB of HBM per device.

v0:
```python
import jax
import jax.numpy as jnp
from jax import lax
from jax.sharding import PartitionSpec as P

epsilon = 1e-06


def shifted(block, axis, distance):
    devices = range(lax.axis_size(axis))
    route = [((i - distance) % len(devices), i) for i in devices]
    return lax.ppermute(block, axis, route)


def unit_rows(x):
    values = x.astype(jnp.float32)
    scale = lax.rsqrt(jnp.sum(values * values, axis=1, keepdims=True) + epsilon)
    return (values * scale, scale)


def norm_back(unit, scale, grad):
    inner = jnp.sum(unit * grad, axis=1, keepdims=True)
    return scale * (grad - unit * inner)


def pair_weights(gathered, match_rows, text_rows, columns, factor, offset):
    logits = lax.dot_general(
        gathered, text_rows, (((1,), (1,)), ((), ())), preferred_element_type=jnp.float32
    )
    logits = factor * logits + offset
    positive = match_rows[:, None] == columns[None, :]
    weight = jnp.where(positive, -jax.nn.sigmoid(-logits), jax.nn.sigmoid(logits))
    return weight.astype(jnp.bfloat16)


def both_grads(weight, gathered, text_rows, factor):
    image_part = factor * jnp.dot(weight, text_rows, preferred_element_type=jnp.float32)
    text_part = factor * lax.dot_general(
        weight, gathered, (((0,), (0,)), ((), ())), preferred_element_type=jnp.float32
    )
    return (image_part, text_part)


def per_device(images, texts, match, logit_scale, logit_bias):
    image_unit, image_scale = unit_rows(images)
    text_unit, text_scale = unit_rows(texts)
    image_send = image_unit.astype(jnp.bfloat16)
    text_send = text_unit.astype(jnp.bfloat16)
    factor = logit_scale[0]
    offset = logit_bias[0]
    gathered, match_rows = (
        lax.all_gather(image_send, "group", axis=0, tiled=True),
        lax.all_gather(match, "group", axis=0, tiled=True),
    )
    cycle_length = lax.axis_size("blk")
    group_count = lax.axis_size("group")
    own_block = lax.axis_index("blk")
    own_group = lax.axis_index("group")
    local_rows = texts.shape[0]
    width = texts.shape[1]
    offsets = jnp.arange(local_rows, dtype=jnp.int32)

    def turn(turn_index, state_carry):
        text_rows, text_total, image_total = state_carry
        source = (own_block - turn_index) % cycle_length
        columns = (source * group_count + own_group) * local_rows + offsets
        weight = pair_weights(gathered, match_rows, text_rows, columns, factor, offset)
        image_part, text_part = both_grads(weight, gathered, text_rows, factor)
        image_total = image_total + image_part
        text_total = shifted(text_total + text_part, "blk", 1)
        text_rows = shifted(text_rows, "blk", 1)
        return (text_rows, text_total, image_total)

    start_state = (
        text_send,
        jnp.zeros((local_rows, width), jnp.float32),
        jnp.zeros(gathered.shape, jnp.float32),
    )
    final_state = lax.fori_loop(0, cycle_length, turn, start_state)
    text_total = final_state[1]
    image_total = final_state[2]
    image_own = lax.psum_scatter(image_total, "group", scatter_dimension=0, tiled=True)
    image_grad = norm_back(image_unit, image_scale, image_own)
    text_grad = norm_back(text_unit, text_scale, text_total)
    return (image_grad, text_grad)


def solution(mesh):
    placed = (P(("blk", "group"), None), P(("blk", "group"), None), P(("blk", "group")), P(), P())
    return jax.shard_map(
        per_device,
        mesh=mesh,
        in_specs=placed,
        out_specs=(P(("blk", "group"), None), P(("blk", "group"), None)),
        check_vma=False,
    )
```

profile of v0, /device:TPU:0, one launch (start us, length us, event | category | flops | bytes accessed | tf_op | source)
XLA Modules:
  0.0 643.7 jit_solution(10818187861560118031)
XLA Ops:
  8.4 1.9 fusion.10
  13.3 12.2 %all-reduce = s32[1408]{0:T(1024)S(1)} all-reduce(s32[1408]{0:T(1024)S(1)} %dynamic-update-slice), channel_id=1, replica_groups=mesh['blk'=16,'group'=8] {'group'}, use_global_device_ids=true, to_apply=%add | all-reduce | flops 1408 | bytes 11264
  27.8 58.4 %all-gather.2.cloned.1.call-done = bf16[1408,1152]{1,0:T(8,128)(2,1)} async-done(((bf16[176,1152]{1,0:T(8,128)(2,1)}), bf16[1408,1152]{1,0:T(8,128)(2,1)}) %all-gather.2.cloned.1.call-update) | async-done | bytes 3244048 | tf_op jit(solution)/shard_map/all_gather | solution.py:52
  86.2 417.6 %while.20 = (s32[]{:T(128)}, bf16[176,1152]{1,0:T(8,128)(2,1)S(1)}, f32[176,1152]{1,0:T(8,128)S(1)}, f32[1408,1152]{1,0:T(8,128)}, f32[]{:T(128)}, /*index=5*/s3...) while((s32[]{:T(128)}, bf16[176,1152]{1,0:T(8,128)(2,1)S(1)}, ...), condition=%wide.region_3.4_spmd.clone, body=%wide.region_2.3_spmd.clone.sunk | while | flops 1720846592 | bytes 42044728 | solution.py:79
  86.3 4.8 select_convert_fusion.2
  91.1 1.6 fusion.39
  92.7 2.8 collective-permute-start
  95.5 4.5 fusion.40
  100.1 12.3 %collective-permute-done = bf16[176,1152]{1,0:T(8,128)(2,1)S(1)} collective-permute-done((bf16[176,1152]{1,0:T(8,128)(2,1)S(1)}, bf16[176,1152]{1,0:T(8,128)(2,1)S(1)}, u32[]{:S(2)}, u32[]{:S(2)}) %collective-permute-start) | collective-permute-done | bytes 405536 | tf_op jit(solution)/shard_map/while/body/eval_jaxpr/ppermute | solution.py:12
  112.4 4.8 select_convert_fusion.2
  117.2 1.6 fusion.39
  119.5 7.4 %fusion.40 = f32[1408,1152]{1,0:T(8,128)} fusion(bf16[1408,176]{0,1:T(8,128)(2,1)S(1)} %select_convert_fusion.2, bf16[176,1152]{1,0:T(8,128)(2,1)S(1)} %copy.13, f32[1408,1152]{1,0:T(8,128)} %get-tuple-element.405, f32[]{:T(128)} %get-tuple-element.422, pred[]{:T(512)S(6)} %compare.4), kind=kOutput, calls=%fused_computation.2.clone.1 | convolution fusion | flops 575815680 | bytes 13877253 | tf_op jit(solution)/shard_map/while/body/eval_jaxpr/dot_general | solution.py:37
  126.9 11.5 %collective-permute-done = bf16[176,1152]{1,0:T(8,128)(2,1)S(1)} collective-permute-done((bf16[176,1152]{1,0:T(8,128)(2,1)S(1)}, bf16[176,1152]{1,0:T(8,128)(2,1)S(1)}, u32[]{:S(2)}, u32[]{:S(2)}) %collective-permute-start) | collective-permute-done | bytes 405536 | tf_op jit(solution)/shard_map/while/body/eval_jaxpr/ppermute | solution.py:12
  138.5 4.8 select_convert_fusion.2
  143.3 1.6 fusion.39
  145.0 7.4 %fusion.40 = f32[1408,1152]{1,0:T(8,128)} fusion(bf16[1408,176]{0,1:T(8,128)(2,1)S(1)} %select_convert_fusion.2, bf16[176,1152]{1,0:T(8,128)(2,1)S(1)} %copy.13, f32[1408,1152]{1,0:T(8,128)} %get-tuple-element.405, f32[]{:T(128)} %get-tuple-element.422, pred[]{:T(512)S(6)} %compare.4), kind=kOutput, calls=%fused_computation.2.clone.1 | convolution fusion | flops 575815680 | bytes 13877253 | tf_op jit(solution)/shard_map/while/body/eval_jaxpr/dot_general | solution.py:37
  152.4 12.1 %collective-permute-done = bf16[176,1152]{1,0:T(8,128)(2,1)S(1)} collective-permute-done((bf16[176,1152]{1,0:T(8,128)(2,1)S(1)}, bf16[176,1152]{1,0:T(8,128)(2,1)S(1)}, u32[]{:S(2)}, u32[]{:S(2)}) %collective-permute-start) | collective-permute-done | bytes 405536 | tf_op jit(solution)/shard_map/while/body/eval_jaxpr/ppermute | solution.py:12
  164.6 4.8 select_convert_fusion.2
  169.4 1.6 fusion.39
  171.1 7.4 %fusion.40 = f32[1408,1152]{1,0:T(8,128)} fusion(bf16[1408,176]{0,1:T(8,128)(2,1)S(1)} %select_convert_fusion.2, bf16[176,1152]{1,0:T(8,128)(2,1)S(1)} %copy.13, f32[1408,1152]{1,0:T(8,128)} %get-tuple-element.405, f32[]{:T(128)} %get-tuple-element.422, pred[]{:T(512)S(6)} %compare.4), kind=kOutput, calls=%fused_computation.2.clone.1 | convolution fusion | flops 575815680 | bytes 13877253 | tf_op jit(solution)/shard_map/while/body/eval_jaxpr/dot_general | solution.py:37
  178.5 12.1 %collective-permute-done = bf16[176,1152]{1,0:T(8,128)(2,1)S(1)} collective-permute-done((bf16[176,1152]{1,0:T(8,128)(2,1)S(1)}, bf16[176,1152]{1,0:T(8,128)(2,1)S(1)}, u32[]{:S(2)}, u32[]{:S(2)}) %collective-permute-start) | collective-permute-done | bytes 405536 | tf_op jit(solution)/shard_map/while/body/eval_jaxpr/ppermute | solution.py:12
  190.7 4.8 select_convert_fusion.2
  197.2 7.4 %fusion.40 = f32[1408,1152]{1,0:T(8,128)} fusion(bf16[1408,176]{0,1:T(8,128)(2,1)S(1)} %select_convert_fusion.2, bf16[176,1152]{1,0:T(8,128)(2,1)S(1)} %copy.13, f32[1408,1152]{1,0:T(8,128)} %get-tuple-element.405, f32[]{:T(128)} %get-tuple-element.422, pred[]{:T(512)S(6)} %compare.4), kind=kOutput, calls=%fused_computation.2.clone.1 | convolution fusion | flops 575815680 | bytes 13877253 | tf_op jit(solution)/shard_map/while/body/eval_jaxpr/dot_general | solution.py:37
  204.6 12.1 %collective-permute-done = bf16[176,1152]{1,0:T(8,128)(2,1)S(1)} collective-permute-done((bf16[176,1152]{1,0:T(8,128)(2,1)S(1)}, bf16[176,1152]{1,0:T(8,128)(2,1)S(1)}, u32[]{:S(2)}, u32[]{:S(2)}) %collective-permute-start) | collective-permute-done | bytes 405536 | tf_op jit(solution)/shard_map/while/body/eval_jaxpr/ppermute | solution.py:12
  216.8 4.8 select_convert_fusion.2
  221.6 1.6 fusion.39
  223.3 7.4 %fusion.40 = f32[1408,1152]{1,0:T(8,128)} fusion(bf16[1408,176]{0,1:T(8,128)(2,1)S(1)} %select_convert_fusion.2, bf16[176,1152]{1,0:T(8,128)(2,1)S(1)} %copy.13, f32[1408,1152]{1,0:T(8,128)} %get-tuple-element.405, f32[]{:T(128)} %get-tuple-element.422, pred[]{:T(512)S(6)} %compare.4), kind=kOutput, calls=%fused_computation.2.clone.1 | convolution fusion | flops 575815680 | bytes 13877253 | tf_op jit(solution)/shard_map/while/body/eval_jaxpr/dot_general | solution.py:37
  230.7 12.1 %collective-permute-done = bf16[176,1152]{1,0:T(8,128)(2,1)S(1)} collective-permute-done((bf16[176,1152]{1,0:T(8,128)(2,1)S(1)}, bf16[176,1152]{1,0:T(8,128)(2,1)S(1)}, u32[]{:S(2)}, u32[]{:S(2)}) %collective-permute-start) | collective-permute-done | bytes 405536 | tf_op jit(solution)/shard_map/while/body/eval_jaxpr/ppermute | solution.py:12
  242.9 4.8 select_convert_fusion.2
  247.7 1.6 fusion.39
  249.4 7.4 %fusion.40 = f32[1408,1152]{1,0:T(8,128)} fusion(bf16[1408,176]{0,1:T(8,128)(2,1)S(1)} %select_convert_fusion.2, bf16[176,1152]{1,0:T(8,128)(2,1)S(1)} %copy.13, f32[1408,1152]{1,0:T(8,128)} %get-tuple-element.405, f32[]{:T(128)} %get-tuple-element.422, pred[]{:T(512)S(6)} %compare.4), kind=kOutput, calls=%fused_computation.2.clone.1 | convolution fusion | flops 575815680 | bytes 13877253 | tf_op jit(solution)/shard_map/while/body/eval_jaxpr/dot_general | solution.py:37
  256.8 12.1 %collective-permute-done = bf16[176,1152]{1,0:T(8,128)(2,1)S(1)} collective-permute-done((bf16[176,1152]{1,0:T(8,128)(2,1)S(1)}, bf16[176,1152]{1,0:T(8,128)(2,1)S(1)}, u32[]{:S(2)}, u32[]{:S(2)}) %collective-permute-start) | collective-permute-done | bytes 405536 | tf_op jit(solution)/shard_map/while/body/eval_jaxpr/ppermute | solution.py:12
  269.0 4.8 select_convert_fusion.2
  273.8 1.6 fusion.39
  275.5 7.4 %fusion.40 = f32[1408,1152]{1,0:T(8,128)} fusion(bf16[1408,176]{0,1:T(8,128)(2,1)S(1)} %select_convert_fusion.2, bf16[176,1152]{1,0:T(8,128)(2,1)S(1)} %copy.13, f32[1408,1152]{1,0:T(8,128)} %get-tuple-element.405, f32[]{:T(128)} %get-tuple-element.422, pred[]{:T(512)S(6)} %compare.4), kind=kOutput, calls=%fused_computation.2.clone.1 | convolution fusion | flops 575815680 | bytes 13877253 | tf_op jit(solution)/shard_map/while/body/eval_jaxpr/dot_general | solution.py:37
  282.9 12.1 %collective-permute-done = bf16[176,1152]{1,0:T(8,128)(2,1)S(1)} collective-permute-done((bf16[176,1152]{1,0:T(8,128)(2,1)S(1)}, bf16[176,1152]{1,0:T(8,128)(2,1)S(1)}, u32[]{:S(2)}, u32[]{:S(2)}) %collective-permute-start) | collective-permute-done | bytes 405536 | tf_op jit(solution)/shard_map/while/body/eval_jaxpr/ppermute | solution.py:12
  295.1 4.8 select_convert_fusion.2
  299.9 1.6 fusion.39
  301.6 7.4 %fusion.40 = f32[1408,1152]{1,0:T(8,128)} fusion(bf16[1408,176]{0,1:T(8,128)(2,1)S(1)} %select_convert_fusion.2, bf16[176,1152]{1,0:T(8,128)(2,1)S(1)} %copy.13, f32[1408,1152]{1,0:T(8,128)} %get-tuple-element.405, f32[]{:T(128)} %get-tuple-element.422, pred[]{:T(512)S(6)} %compare.4), kind=kOutput, calls=%fused_computation.2.clone.1 | convolution fusion | flops 575815680 | bytes 13877253 | tf_op jit(solution)/shard_map/while/body/eval_jaxpr/dot_general | solution.py:37
  309.0 12.1 %collective-permute-done = bf16[176,1152]{1,0:T(8,128)(2,1)S(1)} collective-permute-done((bf16[176,1152]{1,0:T(8,128)(2,1)S(1)}, bf16[176,1152]{1,0:T(8,128)(2,1)S(1)}, u32[]{:S(2)}, u32[]{:S(2)}) %collective-permute-start) | collective-permute-done | bytes 405536 | tf_op jit(solution)/shard_map/while/body/eval_jaxpr/ppermute | solution.py:12
  321.2 4.8 select_convert_fusion.2
  327.7 7.4 %fusion.40 = f32[1408,1152]{1,0:T(8,128)} fusion(bf16[1408,176]{0,1:T(8,128)(2,1)S(1)} %select_convert_fusion.2, bf16[176,1152]{1,0:T(8,128)(2,1)S(1)} %copy.13, f32[1408,1152]{1,0:T(8,128)} %get-tuple-element.405, f32[]{:T(128)} %get-tuple-element.422, pred[]{:T(512)S(6)} %compare.4), kind=kOutput, calls=%fused_computation.2.clone.1 | convolution fusion | flops 575815680 | bytes 13877253 | tf_op jit(solution)/shard_map/while/body/eval_jaxpr/dot_general | solution.py:37
  335.1 12.1 %collective-permute-done = bf16[176,1152]{1,0:T(8,128)(2,1)S(1)} collective-permute-done((bf16[176,1152]{1,0:T(8,128)(2,1)S(1)}, bf16[176,1152]{1,0:T(8,128)(2,1)S(1)}, u32[]{:S(2)}, u32[]{:S(2)}) %collective-permute-start) | collective-permute-done | bytes 405536 | tf_op jit(solution)/shard_map/while/body/eval_jaxpr/ppermute | solution.py:12
  347.3 4.8 select_convert_fusion.2
  353.8 7.4 %fusion.40 = f32[1408,1152]{1,0:T(8,128)} fusion(bf16[1408,176]{0,1:T(8,128)(2,1)S(1)} %select_convert_fusion.2, bf16[176,1152]{1,0:T(8,128)(2,1)S(1)} %copy.13, f32[1408,1152]{1,0:T(8,128)} %get-tuple-element.405, f32[]{:T(128)} %get-tuple-element.422, pred[]{:T(512)S(6)} %compare.4), kind=kOutput, calls=%fused_computation.2.clone.1 | convolution fusion | flops 575815680 | bytes 13877253 | tf_op jit(solution)/shard_map/while/body/eval_jaxpr/dot_general | solution.py:37
  361.2 12.1 %collective-permute-done = bf16[176,1152]{1,0:T(8,128)(2,1)S(1)} collective-permute-done((bf16[176,1152]{1,0:T(8,128)(2,1)S(1)}, bf16[176,1152]{1,0:T(8,128)(2,1)S(1)}, u32[]{:S(2)}, u32[]{:S(2)}) %collective-permute-start) | collective-permute-done | bytes 405536 | tf_op jit(solution)/shard_map/while/body/eval_jaxpr/ppermute | solution.py:12
  373.4 4.8 select_convert_fusion.2
  379.9 7.4 %fusion.40 = f32[1408,1152]{1,0:T(8,128)} fusion(bf16[1408,176]{0,1:T(8,128)(2,1)S(1)} %select_convert_fusion.2, bf16[176,1152]{1,0:T(8,128)(2,1)S(1)} %copy.13, f32[1408,1152]{1,0:T(8,128)} %get-tuple-element.405, f32[]{:T(128)} %get-tuple-element.422, pred[]{:T(512)S(6)} %compare.4), kind=kOutput, calls=%fused_computation.2.clone.1 | convolution fusion | flops 575815680 | bytes 13877253 | tf_op jit(solution)/shard_map/while/body/eval_jaxpr/dot_general | solution.py:37
  387.3 12.1 %collective-permute-done = bf16[176,1152]{1,0:T(8,128)(2,1)S(1)} collective-permute-done((bf16[176,1152]{1,0:T(8,128)(2,1)S(1)}, bf16[176,1152]{1,0:T(8,128)(2,1)S(1)}, u32[]{:S(2)}, u32[]{:S(2)}) %collective-permute-start) | collective-permute-done | bytes 405536 | tf_op jit(solution)/shard_map/while/body/eval_jaxpr/ppermute | solution.py:12
  399.5 4.8 select_convert_fusion.2
  406.0 7.4 %fusion.40 = f32[1408,1152]{1,0:T(8,128)} fusion(bf16[1408,176]{0,1:T(8,128)(2,1)S(1)} %select_convert_fusion.2, bf16[176,1152]{1,0:T(8,128)(2,1)S(1)} %copy.13, f32[1408,1152]{1,0:T(8,128)} %get-tuple-element.405, f32[]{:T(128)} %get-tuple-element.422, pred[]{:T(512)S(6)} %compare.4), kind=kOutput, calls=%fused_computation.2.clone.1 | convolution fusion | flops 575815680 | bytes 13877253 | tf_op jit(solution)/shard_map/while/body/eval_jaxpr/dot_general | solution.py:37
  413.4 12.1 %collective-permute-done = bf16[176,1152]{1,0:T(8,128)(2,1)S(1)} collective-permute-done((bf16[176,1152]{1,0:T(8,128)(2,1)S(1)}, bf16[176,1152]{1,0:T(8,128)(2,1)S(1)}, u32[]{:S(2)}, u32[]{:S(2)}) %collective-permute-start) | collective-permute-done | bytes 405536 | tf_op jit(solution)/shard_map/while/body/eval_jaxpr/ppermute | solution.py:12
  425.6 4.8 select_convert_fusion.2
  432.1 7.4 %fusion.40 = f32[1408,1152]{1,0:T(8,128)} fusion(bf16[1408,176]{0,1:T(8,128)(2,1)S(1)} %select_convert_fusion.2, bf16[176,1152]{1,0:T(8,128)(2,1)S(1)} %copy.13, f32[1408,1152]{1,0:T(8,128)} %get-tuple-element.405, f32[]{:T(128)} %get-tuple-element.422, pred[]{:T(512)S(6)} %compare.4), kind=kOutput, calls=%fused_computation.2.clone.1 | convolution fusion | flops 575815680 | bytes 13877253 | tf_op jit(solution)/shard_map/while/body/eval_jaxpr/dot_general | solution.py:37
  439.5 12.1 %collective-permute-done = bf16[176,1152]{1,0:T(8,128)(2,1)S(1)} collective-permute-done((bf16[176,1152]{1,0:T(8,128)(2,1)S(1)}, bf16[176,1152]{1,0:T(8,128)(2,1)S(1)}, u32[]{:S(2)}, u32[]{:S(2)}) %collective-permute-start) | collective-permute-done | bytes 405536 | tf_op jit(solution)/shard_map/while/body/eval_jaxpr/ppermute | solution.py:12
  451.7 4.8 select_convert_fusion.2
  458.2 7.4 %fusion.40 = f32[1408,1152]{1,0:T(8,128)} fusion(bf16[1408,176]{0,1:T(8,128)(2,1)S(1)} %select_convert_fusion.2, bf16[176,1152]{1,0:T(8,128)(2,1)S(1)} %copy.13, f32[1408,1152]{1,0:T(8,128)} %get-tuple-element.405, f32[]{:T(128)} %get-tuple-element.422, pred[]{:T(512)S(6)} %compare.4), kind=kOutput, calls=%fused_computation.2.clone.1 | convolution fusion | flops 575815680 | bytes 13877253 | tf_op jit(solution)/shard_map/while/body/eval_jaxpr/dot_general | solution.py:37
  465.6 12.1 %collective-permute-done = bf16[176,1152]{1,0:T(8,128)(2,1)S(1)} collective-permute-done((bf16[176,1152]{1,0:T(8,128)(2,1)S(1)}, bf16[176,1152]{1,0:T(8,128)(2,1)S(1)}, u32[]{:S(2)}, u32[]{:S(2)}) %collective-permute-start) | collective-permute-done | bytes 405536 | tf_op jit(solution)/shard_map/while/body/eval_jaxpr/ppermute | solution.py:12
  477.8 4.8 select_convert_fusion.2
  482.5 1.6 fusion.39
  484.3 7.4 %fusion.40 = f32[1408,1152]{1,0:T(8,128)} fusion(bf16[1408,176]{0,1:T(8,128)(2,1)S(1)} %select_convert_fusion.2, bf16[176,1152]{1,0:T(8,128)(2,1)S(1)} %copy.13, f32[1408,1152]{1,0:T(8,128)} %get-tuple-element.405, f32[]{:T(128)} %get-tuple-element.422, pred[]{:T(512)S(6)} %compare.4), kind=kOutput, calls=%fused_computation.2.clone.1 | convolution fusion | flops 575815680 | bytes 13877253 | tf_op jit(solution)/shard_map/while/body/eval_jaxpr/dot_general | solution.py:37
  491.6 12.1 %collective-permute-done = bf16[176,1152]{1,0:T(8,128)(2,1)S(1)} collective-permute-done((bf16[176,1152]{1,0:T(8,128)(2,1)S(1)}, bf16[176,1152]{1,0:T(8,128)(2,1)S(1)}, u32[]{:S(2)}, u32[]{:S(2)}) %collective-permute-start) | collective-permute-done | bytes 405536 | tf_op jit(solution)/shard_map/while/body/eval_jaxpr/ppermute | solution.py:12
  506.2 127.0 %reduce-scatter.2.cloned.1.call-done = f32[176,1152]{1,0:T(8,128)} async-done(((f32[1408,1152]{1,0:T(8,128)}), f32[176,1152]{1,0:T(8,128)}) %reduce-scatter.2.cloned.1.call-update) | async-done | bytes 811024 | tf_op jit(solution)/shard_map/reduce_scatter | solution.py:82
  634.6 2.3 fusion.13
  (139 shorter events, 24.1 us)
Async XLA Ops:
  7.2 79.0 %all-gather.2.cloned.1.call-start = ((), (), s32[]{:S(2)}) async-start(), calls=%async_computation.1 | async-start | bytes 3649536 | tf_op jit(solution)/shard_map/all_gather | solution.py:52
  10.3 622.9 %reduce-scatter.2.cloned.1.call-start = ((), (), s32[]{:S(2)}) async-start(), calls=%async_computation.2 | async-start | bytes 7299072 | tf_op jit(solution)/shard_map/reduce_scatter | solution.py:82
  86.3 4.8 copy-start
  92.6 19.7 %collective-permute-start.1 = (f32[176,1152]{1,0:T(8,128)S(1)}, f32[176,1152]{1,0:T(8,128)S(1)}, u32[]{:S(2)}, u32[]{:S(2)}) collective-permute-start(f32[176,1152]{1,0:T(8,128)S(1)} %fusion.39), channel_id=1, source_target_pairs={{120,0},{0,8},{8,16},{16,24},{24,32},{32,40},{40,48},{48,56},{56,6... | collective-permute-start | bytes 2433032 | tf_op jit(solution)/shard_map/while/body/eval_jaxpr/ppermute | solution.py:12
  92.7 19.6 %collective-permute-start = (bf16[176,1152]{1,0:T(8,128)(2,1)S(1)}, bf16[176,1152]{1,0:T(8,128)(2,1)S(1)}, u32[]{:S(2)}, u32[]{:S(2)}) collective-permute-start(bf16[176,1152]{1,0:T(8,128)(2,1)S(1)} %copy.13), channel_id=1, source_target_pairs={{120,0},{0,8},{8,16},{16,24},{24,32},{32,40},{40,48},{48,56},{56,6... | collective-permute-start | bytes 1216520 | tf_op jit(solution)/shard_map/while/body/eval_jaxpr/ppermute | solution.py:12
  112.4 4.8 copy-start
  118.7 19.7 %collective-permute-start.1 = (f32[176,1152]{1,0:T(8,128)S(1)}, f32[176,1152]{1,0:T(8,128)S(1)}, u32[]{:S(2)}, u32[]{:S(2)}) collective-permute-start(f32[176,1152]{1,0:T(8,128)S(1)} %fusion.39), channel_id=1, source_target_pairs={{120,0},{0,8},{8,16},{16,24},{24,32},{32,40},{40,48},{48,56},{56,6... | collective-permute-start | bytes 2433032 | tf_op jit(solution)/shard_map/while/body/eval_jaxpr/ppermute | solution.py:12
  118.8 19.6 %collective-permute-start = (bf16[176,1152]{1,0:T(8,128)(2,1)S(1)}, bf16[176,1152]{1,0:T(8,128)(2,1)S(1)}, u32[]{:S(2)}, u32[]{:S(2)}) collective-permute-start(bf16[176,1152]{1,0:T(8,128)(2,1)S(1)} %copy.13), channel_id=1, source_target_pairs={{120,0},{0,8},{8,16},{16,24},{24,32},{32,40},{40,48},{48,56},{56,6... | collective-permute-start | bytes 1216520 | tf_op jit(solution)/shard_map/while/body/eval_jaxpr/ppermute | solution.py:12
  138.5 4.8 copy-start
  144.8 19.7 %collective-permute-start.1 = (f32[176,1152]{1,0:T(8,128)S(1)}, f32[176,1152]{1,0:T(8,128)S(1)}, u32[]{:S(2)}, u32[]{:S(2)}) collective-permute-start(f32[176,1152]{1,0:T(8,128)S(1)} %fusion.39), channel_id=1, source_target_pairs={{120,0},{0,8},{8,16},{16,24},{24,32},{32,40},{40,48},{48,56},{56,6... | collective-permute-start | bytes 2433032 | tf_op jit(solution)/shard_map/while/body/eval_jaxpr/ppermute | solution.py:12
  144.9 19.6 %collective-permute-start = (bf16[176,1152]{1,0:T(8,128)(2,1)S(1)}, bf16[176,1152]{1,0:T(8,128)(2,1)S(1)}, u32[]{:S(2)}, u32[]{:S(2)}) collective-permute-start(bf16[176,1152]{1,0:T(8,128)(2,1)S(1)} %copy.13), channel_id=1, source_target_pairs={{120,0},{0,8},{8,16},{16,24},{24,32},{32,40},{40,48},{48,56},{56,6... | collective-permute-start | bytes 1216520 | tf_op jit(solution)/shard_map/while/body/eval_jaxpr/ppermute | solution.py:12
  164.6 4.8 copy-start
  170.9 19.7 %collective-permute-start.1 = (f32[176,1152]{1,0:T(8,128)S(1)}, f32[176,1152]{1,0:T(8,128)S(1)}, u32[]{:S(2)}, u32[]{:S(2)}) collective-permute-start(f32[176,1152]{1,0:T(8,128)S(1)} %fusion.39), channel_id=1, source_target_pairs={{120,0},{0,8},{8,16},{16,24},{24,32},{32,40},{40,48},{48,56},{56,6... | collective-permute-start | bytes 2433032 | tf_op jit(solution)/shard_map/while/body/eval_jaxpr/ppermute | solution.py:12
  171.0 19.6 %collective-permute-start = (bf16[176,1152]{1,0:T(8,128)(2,1)S(1)}, bf16[176,1152]{1,0:T(8,128)(2,1)S(1)}, u32[]{:S(2)}, u32[]{:S(2)}) collective-permute-start(bf16[176,1152]{1,0:T(8,128)(2,1)S(1)} %copy.13), channel_id=1, source_target_pairs={{120,0},{0,8},{8,16},{16,24},{24,32},{32,40},{40,48},{48,56},{56,6... | collective-permute-start | bytes 1216520 | tf_op jit(solution)/shard_map/while/body/eval_jaxpr/ppermute | solution.py:12
  190.7 4.8 copy-start
  197.0 19.7 %collective-permute-start.1 = (f32[176,1152]{1,0:T(8,128)S(1)}, f32[176,1152]{1,0:T(8,128)S(1)}, u32[]{:S(2)}, u32[]{:S(2)}) collective-permute-start(f32[176,1152]{1,0:T(8,128)S(1)} %fusion.39), channel_id=1, source_target_pairs={{120,0},{0,8},{8,16},{16,24},{24,32},{32,40},{40,48},{48,56},{56,6... | collective-permute-start | bytes 2433032 | tf_op jit(solution)/shard_map/while/body/eval_jaxpr/ppermute | solution.py:12
  197.1 19.6 %collective-permute-start = (bf16[176,1152]{1,0:T(8,128)(2,1)S(1)}, bf16[176,1152]{1,0:T(8,128)(2,1)S(1)}, u32[]{:S(2)}, u32[]{:S(2)}) collective-permute-start(bf16[176,1152]{1,0:T(8,128)(2,1)S(1)} %copy.13), channel_id=1, source_target_pairs={{120,0},{0,8},{8,16},{16,24},{24,32},{32,40},{40,48},{48,56},{56,6... | collective-permute-start | bytes 1216520 | tf_op jit(solution)/shard_map/while/body/eval_jaxpr/ppermute | solution.py:12
  216.8 4.8 copy-start
  223.1 19.7 %collective-permute-start.1 = (f32[176,1152]{1,0:T(8,128)S(1)}, f32[176,1152]{1,0:T(8,128)S(1)}, u32[]{:S(2)}, u32[]{:S(2)}) collective-permute-start(f32[176,1152]{1,0:T(8,128)S(1)} %fusion.39), channel_id=1, source_target_pairs={{120,0},{0,8},{8,16},{16,24},{24,32},{32,40},{40,48},{48,56},{56,6... | collective-permute-start | bytes 2433032 | tf_op jit(solution)/shard_map/while/body/eval_jaxpr/ppermute | solution.py:12
  223.2 19.6 %collective-permute-start = (bf16[176,1152]{1,0:T(8,128)(2,1)S(1)}, bf16[176,1152]{1,0:T(8,128)(2,1)S(1)}, u32[]{:S(2)}, u32[]{:S(2)}) collective-permute-start(bf16[176,1152]{1,0:T(8,128)(2,1)S(1)} %copy.13), channel_id=1, source_target_pairs={{120,0},{0,8},{8,16},{16,24},{24,32},{32,40},{40,48},{48,56},{56,6... | collective-permute-start | bytes 1216520 | tf_op jit(solution)/shard_map/while/body/eval_jaxpr/ppermute | solution.py:12
  242.9 4.8 copy-start
  249.2 19.7 %collective-permute-start.1 = (f32[176,1152]{1,0:T(8,128)S(1)}, f32[176,1152]{1,0:T(8,128)S(1)}, u32[]{:S(2)}, u32[]{:S(2)}) collective-permute-start(f32[176,1152]{1,0:T(8,128)S(1)} %fusion.39), channel_id=1, source_target_pairs={{120,0},{0,8},{8,16},{16,24},{24,32},{32,40},{40,48},{48,56},{56,6... | collective-permute-start | bytes 2433032 | tf_op jit(solution)/shard_map/while/body/eval_jaxpr/ppermute | solution.py:12
  249.3 19.6 %collective-permute-start = (bf16[176,1152]{1,0:T(8,128)(2,1)S(1)}, bf16[176,1152]{1,0:T(8,128)(2,1)S(1)}, u32[]{:S(2)}, u32[]{:S(2)}) collective-permute-start(bf16[176,1152]{1,0:T(8,128)(2,1)S(1)} %copy.13), channel_id=1, source_target_pairs={{120,0},{0,8},{8,16},{16,24},{24,32},{32,40},{40,48},{48,56},{56,6... | collective-permute-start | bytes 1216520 | tf_op jit(solution)/shard_map/while/body/eval_jaxpr/ppermute | solution.py:12
  269.0 4.8 copy-start
  275.3 19.7 %collective-permute-start.1 = (f32[176,1152]{1,0:T(8,128)S(1)}, f32[176,1152]{1,0:T(8,128)S(1)}, u32[]{:S(2)}, u32[]{:S(2)}) collective-permute-start(f32[176,1152]{1,0:T(8,128)S(1)} %fusion.39), channel_id=1, source_target_pairs={{120,0},{0,8},{8,16},{16,24},{24,32},{32,40},{40,48},{48,56},{56,6... | collective-permute-start | bytes 2433032 | tf_op jit(solution)/shard_map/while/body/eval_jaxpr/ppermute | solution.py:12
  275.4 19.6 %collective-permute-start = (bf16[176,1152]{1,0:T(8,128)(2,1)S(1)}, bf16[176,1152]{1,0:T(8,128)(2,1)S(1)}, u32[]{:S(2)}, u32[]{:S(2)}) collective-permute-start(bf16[176,1152]{1,0:T(8,128)(2,1)S(1)} %copy.13), channel_id=1, source_target_pairs={{120,0},{0,8},{8,16},{16,24},{24,32},{32,40},{40,48},{48,56},{56,6... | collective-permute-start | bytes 1216520 | tf_op jit(solution)/shard_map/while/body/eval_jaxpr/ppermute | solution.py:12
  295.1 4.8 copy-start
  301.4 19.7 %collective-permute-start.1 = (f32[176,1152]{1,0:T(8,128)S(1)}, f32[176,1152]{1,0:T(8,128)S(1)}, u32[]{:S(2)}, u32[]{:S(2)}) collective-permute-start(f32[176,1152]{1,0:T(8,128)S(1)} %fusion.39), channel_id=1, source_target_pairs={{120,0},{0,8},{8,16},{16,24},{24,32},{32,40},{40,48},{48,56},{56,6... | collective-permute-start | bytes 2433032 | tf_op jit(solution)/shard_map/while/body/eval_jaxpr/ppermute | solution.py:12
  301.5 19.6 %collective-permute-start = (bf16[176,1152]{1,0:T(8,128)(2,1)S(1)}, bf16[176,1152]{1,0:T(8,128)(2,1)S(1)}, u32[]{:S(2)}, u32[]{:S(2)}) collective-permute-start(bf16[176,1152]{1,0:T(8,128)(2,1)S(1)} %copy.13), channel_id=1, source_target_pairs={{120,0},{0,8},{8,16},{16,24},{24,32},{32,40},{40,48},{48,56},{56,6... | collective-permute-start | bytes 1216520 | tf_op jit(solution)/shard_map/while/body/eval_jaxpr/ppermute | solution.py:12
  321.2 4.8 copy-start
  327.5 19.7 %collective-permute-start.1 = (f32[176,1152]{1,0:T(8,128)S(1)}, f32[176,1152]{1,0:T(8,128)S(1)}, u32[]{:S(2)}, u32[]{:S(2)}) collective-permute-start(f32[176,1152]{1,0:T(8,128)S(1)} %fusion.39), channel_id=1, source_target_pairs={{120,0},{0,8},{8,16},{16,24},{24,32},{32,40},{40,48},{48,56},{56,6... | collective-permute-start | bytes 2433032 | tf_op jit(solution)/shard_map/while/body/eval_jaxpr/ppermute | solution.py:12
  327.6 19.6 %collective-permute-start = (bf16[176,1152]{1,0:T(8,128)(2,1)S(1)}, bf16[176,1152]{1,0:T(8,128)(2,1)S(1)}, u32[]{:S(2)}, u32[]{:S(2)}) collective-permute-start(bf16[176,1152]{1,0:T(8,128)(2,1)S(1)} %copy.13), channel_id=1, source_target_pairs={{120,0},{0,8},{8,16},{16,24},{24,32},{32,40},{40,48},{48,56},{56,6... | collective-permute-start | bytes 1216520 | tf_op jit(solution)/shard_map/while/body/eval_jaxpr/ppermute | solution.py:12
  347.3 4.8 copy-start
  353.6 19.7 %collective-permute-start.1 = (f32[176,1152]{1,0:T(8,128)S(1)}, f32[176,1152]{1,0:T(8,128)S(1)}, u32[]{:S(2)}, u32[]{:S(2)}) collective-permute-start(f32[176,1152]{1,0:T(8,128)S(1)} %fusion.39), channel_id=1, source_target_pairs={{120,0},{0,8},{8,16},{16,24},{24,32},{32,40},{40,48},{48,56},{56,6... | collective-permute-start | bytes 2433032 | tf_op jit(solution)/shard_map/while/body/eval_jaxpr/ppermute | solution.py:12
  353.7 19.6 %collective-permute-start = (bf16[176,1152]{1,0:T(8,128)(2,1)S(1)}, bf16[176,1152]{1,0:T(8,128)(2,1)S(1)}, u32[]{:S(2)}, u32[]{:S(2)}) collective-permute-start(bf16[176,1152]{1,0:T(8,128)(2,1)S(1)} %copy.13), channel_id=1, source_target_pairs={{120,0},{0,8},{8,16},{16,24},{24,32},{32,40},{40,48},{48,56},{56,6... | collective-permute-start | bytes 1216520 | tf_op jit(solution)/shard_map/while/body/eval_jaxpr/ppermute | solution.py:12
  373.4 4.8 copy-start
  379.7 19.7 %collective-permute-start.1 = (f32[176,1152]{1,0:T(8,128)S(1)}, f32[176,1152]{1,0:T(8,128)S(1)}, u32[]{:S(2)}, u32[]{:S(2)}) collective-permute-start(f32[176,1152]{1,0:T(8,128)S(1)} %fusion.39), channel_id=1, source_target_pairs={{120,0},{0,8},{8,16},{16,24},{24,32},{32,40},{40,48},{48,56},{56,6... | collective-permute-start | bytes 2433032 | tf_op jit(solution)/shard_map/while/body/eval_jaxpr/ppermute | solution.py:12
  379.8 19.6 %collective-permute-start = (bf16[176,1152]{1,0:T(8,128)(2,1)S(1)}, bf16[176,1152]{1,0:T(8,128)(2,1)S(1)}, u32[]{:S(2)}, u32[]{:S(2)}) collective-permute-start(bf16[176,1152]{1,0:T(8,128)(2,1)S(1)} %copy.13), channel_id=1, source_target_pairs={{120,0},{0,8},{8,16},{16,24},{24,32},{32,40},{40,48},{48,56},{56,6... | collective-permute-start | bytes 1216520 | tf_op jit(solution)/shard_map/while/body/eval_jaxpr/ppermute | solution.py:12
  399.5 4.8 copy-start
  405.8 19.7 %collective-permute-start.1 = (f32[176,1152]{1,0:T(8,128)S(1)}, f32[176,1152]{1,0:T(8,128)S(1)}, u32[]{:S(2)}, u32[]{:S(2)}) collective-permute-start(f32[176,1152]{1,0:T(8,128)S(1)} %fusion.39), channel_id=1, source_target_pairs={{120,0},{0,8},{8,16},{16,24},{24,32},{32,40},{40,48},{48,56},{56,6... | collective-permute-start | bytes 2433032 | tf_op jit(solution)/shard_map/while/body/eval_jaxpr/ppermute | solution.py:12
  405.9 19.6 %collective-permute-start = (bf16[176,1152]{1,0:T(8,128)(2,1)S(1)}, bf16[176,1152]{1,0:T(8,128)(2,1)S(1)}, u32[]{:S(2)}, u32[]{:S(2)}) collective-permute-start(bf16[176,1152]{1,0:T(8,128)(2,1)S(1)} %copy.13), channel_id=1, source_target_pairs={{120,0},{0,8},{8,16},{16,24},{24,32},{32,40},{40,48},{48,56},{56,6... | collective-permute-start | bytes 1216520 | tf_op jit(solution)/shard_map/while/body/eval_jaxpr/ppermute | solution.py:12
  425.5 4.8 copy-start
  431.9 19.7 %collective-permute-start.1 = (f32[176,1152]{1,0:T(8,128)S(1)}, f32[176,1152]{1,0:T(8,128)S(1)}, u32[]{:S(2)}, u32[]{:S(2)}) collective-permute-start(f32[176,1152]{1,0:T(8,128)S(1)} %fusion.39), channel_id=1, source_target_pairs={{120,0},{0,8},{8,16},{16,24},{24,32},{32,40},{40,48},{48,56},{56,6... | collective-permute-start | bytes 2433032 | tf_op jit(solution)/shard_map/while/body/eval_jaxpr/ppermute | solution.py:12
  432.0 19.6 %collective-permute-start = (bf16[176,1152]{1,0:T(8,128)(2,1)S(1)}, bf16[176,1152]{1,0:T(8,128)(2,1)S(1)}, u32[]{:S(2)}, u32[]{:S(2)}) collective-permute-start(bf16[176,1152]{1,0:T(8,128)(2,1)S(1)} %copy.13), channel_id=1, source_target_pairs={{120,0},{0,8},{8,16},{16,24},{24,32},{32,40},{40,48},{48,56},{56,6... | collective-permute-start | bytes 1216520 | tf_op jit(solution)/shard_map/while/body/eval_jaxpr/ppermute | solution.py:12
  451.6 4.8 copy-start
  458.0 19.7 %collective-permute-start.1 = (f32[176,1152]{1,0:T(8,128)S(1)}, f32[176,1152]{1,0:T(8,128)S(1)}, u32[]{:S(2)}, u32[]{:S(2)}) collective-permute-start(f32[176,1152]{1,0:T(8,128)S(1)} %fusion.39), channel_id=1, source_target_pairs={{120,0},{0,8},{8,16},{16,24},{24,32},{32,40},{40,48},{48,56},{56,6... | collective-permute-start | bytes 2433032 | tf_op jit(solution)/shard_map/while/body/eval_jaxpr/ppermute | solution.py:12
  458.1 19.6 %collective-permute-start = (bf16[176,1152]{1,0:T(8,128)(2,1)S(1)}, bf16[176,1152]{1,0:T(8,128)(2,1)S(1)}, u32[]{:S(2)}, u32[]{:S(2)}) collective-permute-start(bf16[176,1152]{1,0:T(8,128)(2,1)S(1)} %copy.13), channel_id=1, source_target_pairs={{120,0},{0,8},{8,16},{16,24},{24,32},{32,40},{40,48},{48,56},{56,6... | collective-permute-start | bytes 1216520 | tf_op jit(solution)/shard_map/while/body/eval_jaxpr/ppermute | solution.py:12
  477.7 4.8 copy-start
  484.1 19.7 %collective-permute-start.1 = (f32[176,1152]{1,0:T(8,128)S(1)}, f32[176,1152]{1,0:T(8,128)S(1)}, u32[]{:S(2)}, u32[]{:S(2)}) collective-permute-start(f32[176,1152]{1,0:T(8,128)S(1)} %fusion.39), channel_id=1, source_target_pairs={{120,0},{0,8},{8,16},{16,24},{24,32},{32,40},{40,48},{48,56},{56,6... | collective-permute-start | bytes 2433032 | tf_op jit(solution)/shard_map/while/body/eval_jaxpr/ppermute | solution.py:12
  484.2 19.6 %collective-permute-start = (bf16[176,1152]{1,0:T(8,128)(2,1)S(1)}, bf16[176,1152]{1,0:T(8,128)(2,1)S(1)}, u32[]{:S(2)}, u32[]{:S(2)}) collective-permute-start(bf16[176,1152]{1,0:T(8,128)(2,1)S(1)} %copy.13), channel_id=1, source_target_pairs={{120,0},{0,8},{8,16},{16,24},{24,32},{32,40},{40,48},{48,56},{56,6... | collective-permute-start | bytes 1216520 | tf_op jit(solution)/shard_map/while/body/eval_jaxpr/ppermute | solution.py:12
  503.8 1.0 copy-start.1
  503.8 129.4 %copy-start.2 = (bf16[176,1152]{1,0:T(8,128)(2,1)S(1)}, bf16[176,1152]{1,0:T(8,128)(2,1)}, u32[]{:S(2)}) copy-start(bf16[176,1152]{1,0:T(8,128)(2,1)} %param.7) | copy-start | bytes 1216516
Sparse Core Ops, SparseCore 0:
  10.4 75.6 all-gather.1
  504.0 129.1 reduce-scatter.1
where the time goes:
time: 646 us; the launch traced here: 644 us
  waiting for transfers between devices  379 us (59%)
  matrix products  216 us (33%)
  between operations  14.8 us (2%)
  blocking collectives  12.2 us (2%)
  other arithmetic  10.5 us (2%)
    ppermute x32, waiting for transfers between devices, shifted(): return lax.ppermute(block, axis, route)  194 us
    reduce_scatter x1, waiting for transfers between devices, per_device(): lax.psum_scatter(image_total, 'group', scatter_dimension=0, tiled=True)  127 us
    dot_general x16, matrix products, both_grads(): jnp.dot(weight, text_rows, preferred_element_type=jnp.float32)  115 us
    dot_general x16, matrix products, pair_weights(): lax.dot_general(gathered, text_rows, (((1,), (1,)), ((), ())), preferred_...  76.2 us
    all_gather x1, waiting for transfers between devices, per_device(): lax.all_gather(image_send, 'group', axis=0, tiled=True)  58.4 us
    dot_general x16, matrix products, both_grads(): lax.dot_general(weight, gathered, (((0,), (0,)), ((), ())), preferred_ele...  24.9 us
  transfers between devices with their start and end apart: 34, of which 18 were waited for; matrix products, arithmetic and copies ran while one was open for 19% of the time, Pallas kernels for 0%

commit v1 on v0

v1 whole, which is shorter than its diff:
```python
import jax
import jax.numpy as jnp
from jax import lax
from jax.experimental import pallas as pl
from jax.experimental.pallas import tpu as pltpu
from jax.sharding import PartitionSpec as P

epsilon = 1e-06
MESH = pl.DeviceIdType.MESH
ROWS, WIDTH = 176, 1152
CUT, HALF_A, HALF_B = 80, 48, 128
A, B = (0, CUT), (CUT, ROWS)
A0, A1, B0, B1 = (0, HALF_A), (HALF_A, CUT), (CUT, HALF_B), (HALF_B, ROWS)
IMAGES, TEXTS = 8 * ROWS, 16 * ROWS
CHUNK = 4 * ROWS
SEMS = 96
bf16, f32 = jnp.bfloat16, jnp.float32


def place():
    b, g = lax.axis_index("blk"), lax.axis_index("group")
    x = lax.rem(b // 2, 2) * 2 + lax.rem(g, 2)
    return x, g // 2, b // 4, lax.rem(b, 2)


def device(x, y, z, core):
    return ((z * 2 + x // 2) * 2 + core, y * 2 + lax.rem(x, 2))


def unit_rows(x):
    values = x.astype(f32)
    scale = lax.rsqrt(jnp.sum(values * values, axis=1, keepdims=True) + epsilon)
    return values * scale, scale


def norm_back(x, grad):
    unit, scale = unit_rows(x)
    inner = jnp.sum(unit * grad, axis=1, keepdims=True)
    return scale * (grad - unit * inner)


class Links:
    def __init__(self, send_sems, recv_sems):
        self.send_sems, self.recv_sems = send_sems, recv_sems
        self.copies, self.sent = {}, 0

    def send(self, name, src, dst, target):
        k = len(self.copies)
        copy = pltpu.make_async_remote_copy(
            src_ref=src, dst_ref=dst, send_sem=self.send_sems.at[k], recv_sem=self.recv_sems.at[k],
            device_id=target, device_id_type=MESH,
        )
        copy.start()
        self.copies[name] = copy

    def arrived(self, *names):
        for name in names:
            self.copies[name].wait_recv()

    def finish(self):
        for copy in list(self.copies.values())[self.sent :]:
            copy.wait_send()
        self.sent = len(self.copies)


class Side:
    def __init__(self, tag, links, up, down, partner, slots, offset):
        self.tag, self.links, self.up, self.down, self.partner = tag, links, up, down, partner
        self.slots, self.offset = slots, offset

    def at(self, ref, r, p, rows):
        return ref.at[pl.ds(self.offset(r, p) + rows[0], rows[1] - rows[0])]

    def send(self, name, src, dst, target):
        self.links.send(self.tag + name, src, dst, target)

    def arrived(self, *names):
        self.links.arrived(*(self.tag + n for n in names))

    def gather_start(self):
        at, s = self.at, self.slots
        self.send("gB", at(s, 0, 0, B), at(s, 0, 1, B), self.partner)
        self.send("gA3", at(s, 0, 0, A), at(s, 3, 0, A), self.up)
        self.send("gA1", at(s, 0, 0, A), at(s, 1, 0, A), self.down)
        self.send("gB3", at(s, 0, 0, B), at(s, 3, 0, B), self.up)
        self.send("gB1", at(s, 0, 0, B), at(s, 1, 0, B), self.down)
        self.send("gA", at(s, 0, 0, A), at(s, 0, 1, A), self.partner)

    def gather_pair(self):
        at, s = self.at, self.slots
        self.arrived("gB")
        self.send("gC3", at(s, 0, 1, B), at(s, 3, 1, B), self.up)
        self.send("gC1", at(s, 0, 1, B), at(s, 1, 1, B), self.down)

    def gather_a(self):
        at, s = self.at, self.slots
        self.arrived("gA1", "gA3")
        self.send("gA20", at(s, 1, 0, A0), at(s, 2, 0, A0), self.down)
        self.send("gA21", at(s, 3, 0, A1), at(s, 2, 0, A1), self.up)
        self.send("gD1", at(s, 1, 0, A), at(s, 1, 1, A), self.partner)
        self.send("gD3", at(s, 3, 0, A), at(s, 3, 1, A), self.partner)

    def gather_b(self):
        at, s = self.at, self.slots
        self.arrived("gB1", "gB3")
        self.send("gB20", at(s, 1, 0, B0), at(s, 2, 0, B0), self.down)
        self.send("gB21", at(s, 3, 0, B1), at(s, 2, 0, B1), self.up)

    def gather_a2(self):
        at, s = self.at, self.slots
        self.arrived("gA20", "gA21")
        self.send("gD2", at(s, 2, 0, A), at(s, 2, 1, A), self.partner)

    def gather_c(self):
        at, s = self.at, self.slots
        self.arrived("gC1", "gC3")
        self.send("gC20", at(s, 1, 1, B0), at(s, 2, 1, B0), self.down)
        self.send("gC21", at(s, 3, 1, B1), at(s, 2, 1, B1), self.up)

    def sum_refs(self, pair_a, half, ring):
        self.pair_a, self.half, self.ring = pair_a, half, ring

    def rows_of(self, r, p, rows):
        return pl.ds(self.offset(r, p) + rows[0], rows[1] - rows[0])

    def mine(self, r, p, rows):
        return self.slots.at[self.rows_of(r, p, rows)]

    def pair_slot(self, r):
        return pl.ds(r * CUT, CUT)

    def half_slot(self, kind, rows):
        base = 0 if kind == 0 else CUT + (kind - 1) * (ROWS - CUT) - CUT
        return pl.ds(base + rows[0], rows[1] - rows[0])

    def ring_slot(self, r, p, rows):
        return pl.ds((r * 2 + p) * ROWS + rows[0], rows[1] - rows[0])

    def add(self, rows, *pieces):
        total = self.slots[rows, :].astype(f32)
        for ref, where in pieces:
            total = total + ref[where, :].astype(f32)
        self.slots[rows, :] = total.astype(bf16)

    def sum_far(self):
        self.send("sX2", self.mine(2, 1, A), self.pair_a.at[self.pair_slot(2)], self.partner)
        for p in (0, 1):
            self.send(f"sH0{p}", self.mine(2, p, B0), self.half.at[self.half_slot(1 + p, B0)], self.up)
            self.send(f"sH1{p}", self.mine(2, p, B1), self.half.at[self.half_slot(1 + p, B1)], self.down)

    def sum_far_a(self):
        self.arrived("sX2")
        self.add(self.rows_of(2, 0, A), (self.pair_a, self.pair_slot(2)))
        self.send("sHA0", self.mine(2, 0, A0), self.half.at[self.half_slot(0, A0)], self.up)
        self.send("sHA1", self.mine(2, 0, A1), self.half.at[self.half_slot(0, A1)], self.down)

    def sum_near(self, r):
        h, rows, target, slot = ("0", B0, self.up, 0) if r == 1 else ("1", B1, self.down, 1)
        self.send(f"sX{r}", self.mine(r, 1, A), self.pair_a.at[self.pair_slot(r)], self.partner)
        for p in (0, 1):
            self.arrived(f"sH{h}{p}")
            self.add(self.rows_of(r, p, rows), (self.half, self.half_slot(1 + p, rows)))
            self.send(f"sR{r}{p}", self.mine(r, p, B), self.ring.at[self.ring_slot(slot, p, B)], target)

    def sum_near_a(self, r):
        h, rows, target, slot = ("0", A0, self.up, 0) if r == 1 else ("1", A1, self.down, 1)
        self.arrived(f"sX{r}", f"sHA{h}")
        self.add(self.rows_of(r, 0, A), (self.pair_a, self.pair_slot(r)))
        self.add(self.rows_of(r, 0, rows), (self.half, self.half_slot(0, rows)))
        self.send(f"sRA{r}", self.mine(r, 0, A), self.ring.at[self.ring_slot(slot, 0, A)], target)

    def sum_own(self):
        self.send("sX0", self.mine(0, 1, A), self.pair_a.at[self.pair_slot(0)], self.partner)

    def sum_own_b(self):
        self.arrived("sR11", "sR31")
        self.add(self.rows_of(0, 1, B), (self.ring, self.ring_slot(0, 1, B)), (self.ring, self.ring_slot(1, 1, B)))
        self.send("sXB", self.mine(0, 1, B), self.pair_a.at[pl.ds(4 * CUT, ROWS - CUT)], self.partner)

    def total(self, own):
        self.arrived("sX0", "sRA1", "sRA3", "sR10", "sR30", "sXB")
        rest = self.ring[self.ring_slot(0, 0, (0, ROWS)), :].astype(f32)
        rest = rest + self.ring[self.ring_slot(1, 0, (0, ROWS)), :].astype(f32)
        first = self.pair_a[self.pair_slot(0), :].astype(f32)
        last = self.pair_a[pl.ds(4 * CUT, ROWS - CUT), :].astype(f32)
        return own + rest + jnp.concatenate([first, last], axis=0)


def dot(a, b, ca, cb):
    return lax.dot_general(a, b, (((ca,), (cb,)), ((), ())), preferred_element_type=f32)


def kernel(
    images, texts, matches, scale_ref, bias_ref, image_grad, text_grad,
    i_slots, t_slots, m_slots, where_ref, di, dt, t_sib,
    i_pair, t_pair, i_half, t_half, i_ring, t_ring, send_sems, recv_sems,
):
    x, y, z, core = place()
    odd = lax.rem(x, 2)
    xi = x + 1 - 2 * odd
    xt = lax.rem(x + 3 + 2 * odd, 4)
    y_up, y_down, y_far = lax.rem(y + 1, 4), lax.rem(y + 3, 4), lax.rem(y + 2, 4)
    z_up, z_down = lax.rem(z + 1, 4), lax.rem(z + 3, 4)
    sibling = device(x, y, z, 1 - core)
    peers = {(r, p): device((x, xi)[p], (y, y_up, y_far, y_down)[r], z, core) for r in range(4) for p in range(2)}
    up_t, down_t = device(x, y, z_up, core), device(x, y, z_down, core)
    pair_t = device(xt, y, z, core)

    barrier = pltpu.get_barrier_semaphore()
    greeted = [d for k, d in peers.items() if k != (0, 0)] + [up_t, down_t, pair_t, sibling]
    for d in greeted:
        pl.semaphore_signal(barrier, inc=1, device_id=d, device_id_type=MESH)
    i_slots[pl.ds(0, ROWS), :] = unit_rows(images[...])[0].astype(bf16)
    t_slots[pl.ds(0, ROWS), :] = unit_rows(texts[...])[0].astype(bf16)
    m_slots[0] = matches[0]
    pl.semaphore_wait(barrier, len(greeted))

    links = Links(send_sems, recv_sems)
    im = Side("i", links, peers[1, 0], peers[3, 0], peers[0, 1], i_slots, lambda r, p: (r * 2 + p) * ROWS)
    te = Side("t", links, up_t, down_t, pair_t, t_slots, lambda r, p: (r * 4 + p) * ROWS)
    im.sum_refs(i_pair, i_half, i_ring)
    te.sum_refs(t_pair, t_half, t_ring)
    both = (im, te)

    def to_sibling(r):
        links.send(f"sib{r}", t_slots.at[pl.ds(r * CHUNK, 2 * ROWS)], t_slots.at[pl.ds(r * CHUNK + 2 * ROWS, 2 * ROWS)], sibling)

    for side in both:
        side.gather_start()
    for r in range(4):
        for p in range(2):
            if (r, p) != (0, 0):
                k = ((4 - r) % 4) * 2 + p
                links.send(f"m{k}", matches.at[k], m_slots.at[k], peers[r, p])
    for side in both:
        side.gather_pair()
    for side in both:
        side.gather_a()
    for side in both:
        side.gather_b()
    te.arrived("gA")
    to_sibling(0)
    for side in both:
        side.gather_a2()
    for side in both:
        side.gather_c()

    links.arrived(*(f"m{k}" for k in range(1, 8)))
    match = m_slots[0]
    for k in range(1, 8):
        match = match + m_slots[k]
    owner = ((match.astype(f32) + 0.5) * (1.0 / ROWS)).astype(jnp.int32)
    b, g = owner >> 3, owner & 7
    ox = ((b >> 1) & 1) * 2 + (g & 1)
    held = ((g >> 1) == y) & ((ox == x) | (ox == xt))
    slot = (((b >> 2) - z + 4) & 3) * 4 + jnp.where((b & 1) == core, 0, 2) + jnp.where(ox == x, 0, 1)
    where_ref[...] = jnp.where(held, slot * ROWS + match - owner * ROWS, -1)

    im.arrived("gA", "gD1", "gD3")
    te.arrived("gD1", "gD3")
    to_sibling(1)
    to_sibling(3)
    for side in both:
        side.arrived("gB20", "gB21", "gC20", "gC21", "gD2")
    to_sibling(2)

    factor, bias = scale_ref[0], bias_ref[0]

    def block(r, first):
        t = t_slots[pl.ds(r * CHUNK, CHUNK), :]
        i = i_slots[...]
        logits = factor * dot(t, i, 1, 1) + bias
        here = where_ref[...] == lax.broadcasted_iota(jnp.int32, (CHUNK, IMAGES), 0) + r * CHUNK
        w = 1.0 / (1.0 + jnp.exp(jnp.where(here, logits, -logits)))
        w = jnp.where(here, -w, w).astype(bf16)
        d = dot(w, i, 1, 0)
        g = dot(w, t, 0, 0)
        if r == 0:
            dt[...] = d[:ROWS]
        t_slots[pl.ds(r * CHUNK, CHUNK), :] = d.astype(bf16)
        links.send(
            f"back{r}", t_slots.at[pl.ds(r * CHUNK + 2 * ROWS, 2 * ROWS)], t_sib.at[pl.ds(r * 2 * ROWS, 2 * ROWS)], sibling
        )
        if first:
            di[...] = g
        else:
            di[...] += g

    def from_sibling(r):
        links.arrived(f"back{r}")
        te.add(pl.ds(r * CHUNK, 2 * ROWS), (t_sib, pl.ds(r * 2 * ROWS, 2 * ROWS)))

    links.finish()
    links.arrived("sib2")
    block(2, True)
    from_sibling(2)
    te.sum_far()
    links.arrived("sib1")
    block(1, False)
    from_sibling(1)
    te.sum_far_a()
    te.sum_near(1)
    links.arrived("sib3")
    block(3, False)
    from_sibling(3)
    te.sum_near(3)
    te.sum_near_a(1)
    te.sum_near_a(3)
    links.arrived("sib0")
    block(0, False)
    i_slots[...] = di[...].astype(bf16)
    im.sum_far()
    from_sibling(0)
    te.sum_own()
    te.sum_own_b()
    im.sum_far_a()
    im.sum_near(1)
    im.sum_near(3)
    im.sum_near_a(1)
    im.sum_near_a(3)
    im.sum_own()
    own = dt[...] + t_sib[pl.ds(0, ROWS), :].astype(f32)
    text_grad[...] = norm_back(texts[...], factor * te.total(own))
    im.sum_own_b()
    image_grad[...] = norm_back(images[...], factor * im.total(di[pl.ds(0, ROWS), :]))
    links.finish()


def per_device(images, texts, match, logit_scale, logit_bias):
    spread = jnp.eye(8, dtype=jnp.int32)[:, :, None] * match[None, None, :]
    vmem = pl.BlockSpec(memory_space=pltpu.VMEM)
    smem = pl.BlockSpec(memory_space=pltpu.SMEM)
    rows = lambda n: pltpu.VMEM((n, WIDTH), bf16)
    return pl.pallas_call(
        kernel,
        out_shape=(jax.ShapeDtypeStruct((ROWS, WIDTH), f32), jax.ShapeDtypeStruct((ROWS, WIDTH), f32)),
        in_specs=[vmem, vmem, vmem, smem, smem],
        out_specs=(vmem, vmem),
        scratch_shapes=[
            rows(IMAGES), rows(TEXTS), pltpu.VMEM((8, 1, IMAGES), jnp.int32), pltpu.VMEM((1, IMAGES), jnp.int32),
            pltpu.VMEM((IMAGES, WIDTH), f32), pltpu.VMEM((ROWS, WIDTH), f32), rows(IMAGES),
            rows(4 * CUT + ROWS - CUT), rows(4 * CUT + ROWS - CUT),
            rows(2 * ROWS - CUT), rows(2 * ROWS - CUT), rows(4 * ROWS), rows(4 * ROWS),
            pltpu.SemaphoreType.DMA((SEMS,)), pltpu.SemaphoreType.DMA((SEMS,)),
        ],
        compiler_params=pltpu.CompilerParams(collective_id=0, has_side_effects=True, vmem_limit_bytes=62 << 20),
        cost_estimate=pl.CostEstimate(
            flops=6 * IMAGES * TEXTS * WIDTH, bytes_accessed=8 * ROWS * WIDTH, transcendentals=2 * IMAGES * TEXTS
        ),
        name="contrastive",
    )(images, texts, spread.reshape(8, 1, IMAGES), logit_scale, logit_bias)


def solution(mesh):
    rows = P(("blk", "group"), None)
    return jax.shard_map(
        per_device,
        mesh=mesh,
        in_specs=(rows, rows, P(("blk", "group")), P(), P()),
        out_specs=(rows, rows),
        check_vma=False,
    )
```

time: 646 us -> 121 us (0.19)
  waiting for transfers between devices: 379 us -> 0 us
  matrix products: 216 us -> 0 us
  Pallas kernels: 0 us -> 114 us
  between operations: 14.8 us -> 1.97 us
  blocking collectives: 12.2 us -> 0 us
  other arithmetic: 10.5 us -> 0.66 us
    dot_general x48 -> x0, matrix products: 216 us -> none  [the longest x16 115 us: both_grads(): jnp.dot(weight, text_rows, preferred_element_type=jnp.float32)]
    ppermute x32 -> x0, waiting for transfers between devices: 194 us -> none  [shifted(): return lax.ppermute(block, axis, route)]
    reduce_scatter x1 -> x0, waiting for transfers between devices: 127 us -> none  [per_device(): lax.psum_scatter(image_total, 'group', scatter_dimension=0, tiled=True)]
    pallas_call x0 -> x1, Pallas kernels: none -> 114 us  [per_device(): pl.pallas_call(kernel, out_shape=(jax.ShapeDtypeStruct((ROWS, WIDTH), f32...]
    all_gather x1 -> x0, waiting for transfers between devices: 58.4 us -> none  [per_device(): lax.all_gather(image_send, 'group', axis=0, tiled=True)]
    unnamed x1 -> x0, blocking collectives: 12.2 us -> none
  transfers between devices with their start and end apart: 34 -> 0, of which waited for: 18 -> 0; matrix products, arithmetic and copies ran while one was open for 19% -> 0% of each run, Pallas kernels for 0% -> 0%
where the time goes in v1:
time: 121 us; the launch traced here: 120 us
  Pallas kernels  114 us (94%)
  local copies, waits for them, and re-layouts  4 us (3%)
  between operations  1.97 us (2%)
    pallas_call x1, Pallas kernels, per_device(): pl.pallas_call(kernel, out_shape=(jax.ShapeDtypeStruct((ROWS, WIDTH), f32...  114 us
    unnamed x6, local copies, waits for them, and re-layouts  3.71 us

profile of v1, /device:TPU:0, one launch (start us, length us, event | category | flops | bytes accessed | tf_op | source)
XLA Modules:
  0.0 120.5 jit_solution(4073312141185081890)
XLA Ops:
  1.9 0.0 copy-start.1
  1.9 0.7 copy-done.1
  2.6 0.1 mul.29
  2.7 0.1 mul.26
  2.8 0.1 mul.27
  2.9 0.7 broadcast_multiply_fusion.matches
  3.6 113.8 %contrastive.1 = (f32[176,1152]{1,0:T(8,128)}, f32[176,1152]{1,0:T(8,128)}) custom-call(bf16[176,1152]{1,0:T(8,128)(2,1)} %images.1, bf16[176,1152]{1,0:T(8,128)(2,1)} %texts.1, s32[8,1,1408]{2,1,0:T(1,128)} %broadcast_multiply_fusion.matches, f32[1]{0:T(128)S(6)} %copy.9.scale_ref, f32[1]{0:T(128)S(6)} %copy.10.bias_ref), custom_call_target="tpu_custom_call" | custom-call | flops 27405582336 | bytes 1622016 | tf_op jit(solution)/shard_map/contrastive/pallas_call | solution.py:334
  117.4 0.0 copy-start
  117.4 2.2 %copy.11 = f32[176,1152]{1,0:T(8,128)} copy(f32[176,1152]{1,0:T(8,128)} %get-tuple-element.4) | data formatting | bytes 1622016
  119.6 0.0 copy-done
  119.6 0.9 copy.12
  (2 shorter events, 0.0 us)
Async XLA Ops:
  1.9 0.7 copy-start.1
  117.4 2.2 %copy-start = (f32[176,1152]{1,0:T(8,128)S(1)}, f32[176,1152]{1,0:T(8,128)}, u32[]{:S(2)}) copy-start(f32[176,1152]{1,0:T(8,128)} %get-tuple-element.5) | copy-start | bytes 2433028
